TPU v7x, 32 devices: a whole 2x2x4 slice. The times are simulated.
32 devices in a mesh: dp: 8 (over z, y), seq: 4 (over x, core).
Axes of the slice: x: 2, y: 2, z: 4, core: 2. Of those that a mesh axis runs over, the one named last changes fastest.
Arguments:
- inputs: bfloat16 [16, 2048, 768], P('dp', 'seq'), may hold values from -6 to 6
- conv_weight: bfloat16 [3, 768, 384], P(None, 'dp', 'seq'), may hold values from -0.125 to 0.125
- point_weight: bfloat16 [384, 768], P('seq', 'dp'), may hold values from -0.3125 to 0.3125
- cotangent: bfloat16 [16, 2048, 768], P('dp', 'seq'), may hold values from -6 to 6
Outputs:
- input_grad: bfloat16 [16, 2048, 768], P('dp', 'seq')
- conv_grad: float32 [3, 768, 384], P(None, 'dp', 'seq')
All inputs are finite; a program needn't handle non-finite values.
Results may differ from a plain program's by a relative error of at most 0.0054.
Values may be sent and summed in bfloat16 or wider, within the bound.
A program may use at most 64 MiB of HBM per device.

v0:
```python
import jax
import jax.numpy as jnp
from jax import lax
from jax.sharding import PartitionSpec as P

SPAN = 2


EPSILON = 1e-06
GELU_SCALE = 0.7978845608028654
GELU_CUBIC = 0.044715


def from_behind(x, axis, by):
    peers = lax.axis_size(axis)
    pairs = [(i, i + by) for i in range(peers) if 0 <= i + by < peers]
    return lax.ppermute(x, axis, pairs)


def gelu_tanh(values):
    return (
        0.5
        * values
        * (1.0 + jnp.tanh(GELU_SCALE * (values + GELU_CUBIC * values * values * values)))
    )


def gelu_slope(values):
    tangent = jnp.tanh(GELU_SCALE * (values + GELU_CUBIC * values * values * values))
    return 0.5 * (1.0 + tangent) + 0.5 * values * (1.0 - tangent * tangent) * GELU_SCALE * (
        1.0 + 3.0 * GELU_CUBIC * values * values
    )


def product(left, right):
    return jnp.dot(left, right, preferred_element_type=jnp.float32)


def outer_sum(left, right):
    return jnp.einsum("rc,rf->cf", left, right, preferred_element_type=jnp.float32)


def to_half(values):
    return lax.optimization_barrier(values.astype(jnp.bfloat16))


def from_lower(array):
    moved = from_behind(array, "seq", SPAN)
    return moved


def from_upper(array):
    moved = from_behind(array, "seq", -SPAN)
    return moved


def body(inputs, conv_weight, point_weight, cotangent):
    samp_count, bin_count, width = inputs.shape
    row_count = samp_count * bin_count
    grad_scale = float(row_count * lax.axis_size("dp") * lax.axis_size("seq")) ** (-0.5)
    columns = (
        lax.all_gather(conv_weight, "seq", axis=2, tiled=True),
        lax.all_gather(point_weight, "seq", axis=0, tiled=True),
    )
    conv_full, point_full = (
        lax.all_gather(columns[0], "dp", axis=1, tiled=True),
        lax.all_gather(columns[1], "dp", axis=1, tiled=True),
    )
    hidden = conv_full.shape[2]
    floats = inputs.astype(jnp.float32)
    row_scale = lax.rsqrt(jnp.mean(floats * floats, axis=-1, keepdims=True) + EPSILON)
    normed = floats * row_scale
    acted = gelu_tanh(normed).astype(jnp.bfloat16)
    acted_flat = acted.reshape(row_count, width)
    lower_acts = from_lower(acted).reshape(row_count, width)
    upper_acts = from_upper(acted).reshape(row_count, width)
    shifted_low = to_half(product(lower_acts, conv_full[0])).astype(jnp.float32)
    shifted_high = to_half(product(upper_acts, conv_full[2])).astype(jnp.float32)
    preact = shifted_low + product(acted_flat, conv_full[1]) + shifted_high
    cot_flat = cotangent.reshape(row_count, width)
    grad_inner = product(cot_flat, point_full.T)
    grad_pre = (grad_inner * gelu_slope(preact)).astype(jnp.bfloat16)
    grad_blocks = grad_pre.reshape(samp_count, bin_count, hidden)
    grad_upper = from_upper(grad_blocks).reshape(row_count, hidden)
    grad_lower = from_lower(grad_blocks).reshape(row_count, hidden)
    grad_act = (
        product(grad_upper, conv_full[0].T)
        + product(grad_pre, conv_full[1].T)
        + product(grad_lower, conv_full[2].T)
    )
    normed_flat = normed.reshape(row_count, width)
    scale_flat = row_scale.reshape(row_count, 1)
    grad_norm = grad_act * gelu_slope(normed_flat)
    center = jnp.mean(grad_norm * normed_flat, axis=-1, keepdims=True)
    grad_input = cot_flat.astype(jnp.float32) + scale_flat * (grad_norm - normed_flat * center)
    input_grad = grad_input.astype(jnp.bfloat16).reshape(samp_count, bin_count, width)
    conv_terms = (
        jnp.stack(
            [
                outer_sum(acted_flat, grad_upper),
                outer_sum(acted_flat, grad_pre),
                outer_sum(acted_flat, grad_lower),
            ],
            axis=0,
        )
        * grad_scale
    )
    partial_terms = lax.psum_scatter(conv_terms, "dp", scatter_dimension=1, tiled=True)
    conv_grad = lax.psum_scatter(partial_terms, "seq", scatter_dimension=2, tiled=True)
    return (input_grad, conv_grad)


def solution(mesh):
    return jax.shard_map(
        body,
        mesh=mesh,
        in_specs=(P("dp", "seq", None), P(None, "dp", "seq"), P("seq", "dp"), P("dp", "seq", None)),
        out_specs=(P("dp", "seq", None), P(None, "dp", "seq")),
        check_vma=False,
    )
```

profile of v0, /device:TPU:0, one launch (start us, length us, event | category | flops | bytes accessed | tf_op | source)
XLA Modules:
  0.0 246.5 jit_solution(7921569443818153190)
XLA Ops:
  7.2 0.0 all-gather.2.cloned.1.call-start
  7.2 1.0 copy.18
  8.2 7.9 %all_gather.14 = bf16[3,96,384]{1,0,2:T(4,128)(2,1)S(1)} all-gather(bf16[3,96,96]{1,0,2:T(4,128)(2,1)S(1)} %copy.18), channel_id=1, replica_groups=mesh['dp'=8,'seq'=4] {'seq'}, dimensions={2}, use_global_device_ids=true | all-gather | bytes 276480 | tf_op jit(solution)/shard_map/all_gather | solution.py:62
  16.1 0.9 copy.19
  17.0 0.0 all-gather.2.cloned.1.call-update
  17.1 0.0 reduce-scatter.5.cloned.1.call-start
  17.1 0.0 copy-start
  17.1 1.9 fusion
  19.1 0.0 copy-done
  19.1 0.0 copy-start.7
  19.1 2.4 fusion.5
  21.5 1.3 collective-permute-start.1
  22.7 6.8 %collective-permute-start = (bf16[2,512,768]{2,1,0:T(8,128)(2,1)}, bf16[2,512,768]{2,1,0:T(8,128)(2,1)}, u32[]{:S(2)}, u32[]{:S(2)}) collective-permute-start(bf16[2,512,768]{2,1,0:T(8,128)(2,1)} %get-tuple-element.2), channel_id=1, source_target_pairs={{0,2},{1,3},{4,6},{5,7},{8,10},{9,11},{12,14},{13,15},{16,18},{17,... | collective-permute-start | bytes 4718600 | tf_op jit(solution)/shard_map/ppermute | solution.py:17
  29.6 0.0 copy-done.7
  29.6 33.4 %all_gather.12 = bf16[384,96]{1,0:T(8,128)(2,1)S(1)} all-gather(bf16[96,96]{1,0:T(8,128)(2,1)S(1)} %copy-done.7), channel_id=1, replica_groups=mesh['dp'=8,'seq'=4] {'seq'}, dimensions={0}, use_global_device_ids=true | all-gather | bytes 92160 | tf_op jit(solution)/shard_map/all_gather | solution.py:63
  63.0 0.1 copy.17
  63.2 31.9 %all_gather.13 = bf16[384,768]{0,1:T(8,128)(2,1)S(1)} all-gather(bf16[384,96]{0,1:T(8,128)(2,1)S(1)} %copy.17), channel_id=1, replica_groups=mesh['dp'=8,'seq'=4] {'dp'}, dimensions={1}, use_global_device_ids=true | all-gather | bytes 663552 | tf_op jit(solution)/shard_map/all_gather | solution.py:67
  95.0 3.5 %fusion.31 = f32[1024,384]{1,0:T(8,128)} fusion(bf16[1024,768]{1,0:T(8,128)(2,1)} %bitcast.79, bf16[384,768]{0,1:T(8,128)(2,1)S(1)} %all_gather.13), kind=kOutput, calls=%fused_computation.52 | convolution fusion | flops 603979776 | bytes 3735552 | tf_op jit(solution)/shard_map/dot_general | solution.py:36
  98.6 0.0 collective-permute-done.1
  98.6 0.0 all-gather.2.cloned.1.call-done
  98.6 0.0 copy-start.4
  98.6 2.6 %convolution_convert_fusion = bf16[1024,384]{1,0:T(8,128)(2,1)S(1)} fusion(bf16[1024,768]{1,0:T(8,128)(2,1)} %bitcast.5, bf16[3,768,384]{2,1,0:T(8,128)(2,1)} %all-gather.2.cloned.1.call-done), kind=kOutput, calls=%fused_computation.37 | convolution fusion | flops 604372992 | bytes 2949120 | tf_op jit(solution)/shard_map/dot_general | solution.py:36
  101.2 0.0 collective-permute-done
  101.2 0.0 copy-done.4
  101.3 2.4 convolution_convert_fusion.1
  103.6 0.0 copy-start.2
  103.6 2.5 %fusion.28 = f32[1024,384]{1,0:T(8,128)S(1)} fusion(bf16[1024,768]{1,0:T(8,128)(2,1)} %bitcast.3, bf16[3,768,384]{2,1,0:T(8,128)(2,1)S(1)} %copy-done.4), kind=kOutput, calls=%fused_computation.47 | convolution fusion | flops 603979776 | bytes 3735552 | tf_op jit(solution)/shard_map/dot_general | solution.py:36
  106.2 0.0 copy-done.2
  106.2 1.2 fusion.25
  107.4 0.0 copy-start.1
  107.4 1.3 collective-permute-start.2
  108.7 5.4 %collective-permute-start.3 = (bf16[2,512,384]{2,1,0:T(8,128)(2,1)S(1)}, bf16[2,512,384]{2,1,0:T(8,128)(2,1)S(1)}, u32[]{:S(2)}, u32[]{:S(2)}) collective-permute-start(bf16[2,512,384]{2,1,0:T(8,128)(2,1)S(1)} %bitcast.78), channel_id=1, source_target_pairs={{0,2},{1,3},{4,6},{5,7},{8,10},{9,11},{12,14},{13,15},{16,18},{17,... | collective-permute-start | bytes 2359304 | tf_op jit(solution)/shard_map/ppermute | solution.py:17
  114.1 2.4 convolution_bitcast_fusion.1
  116.6 0.0 copy-done.1
  116.6 7.4 %collective-permute-done.2 = bf16[2,512,384]{2,1,0:T(8,128)(2,1)S(1)} collective-permute-done((bf16[2,512,384]{2,1,0:T(8,128)(2,1)S(1)}, bf16[2,512,384]{2,1,0:T(8,128)(2,1)S(1)}, u32[]{:S(2)}, u32[]{:S(2)}) %collective-permute-start.2) | collective-permute-done | bytes 786464 | tf_op jit(solution)/shard_map/ppermute | solution.py:17
  123.9 0.0 copy-start.5
  123.9 2.7 %convolution_bitcast_fusion.2 = f32[1,768,384]{2,1,0:T(8,128)S(1)} fusion(bf16[2,512,768]{2,1,0:T(8,128)(2,1)} %get-tuple-element.2, bf16[2,512,384]{2,1,0:T(8,128)(2,1)S(1)} %collective-permute-done.2), kind=kOutput, calls=%fused_computation.41 | convolution fusion | flops 603979776 | bytes 3538944 | tf_op jit(solution)/shard_map/rc,rf->cf/dot_general | solution.py:40
  126.6 0.0 copy-done.5
  126.6 0.0 collective-permute-done.3
  126.7 0.0 copy-start.8
  126.7 0.9 copy-done.8
  127.6 2.4 convolution_bitcast_fusion
  130.0 2.1 maximum_multiply_fusion
  132.0 0.0 reduce-scatter.5.cloned.1.call-update
  132.0 0.2 reduce-scatter.7.cloned.1.call-start
  132.3 0.0 copy-start.6
  132.3 4.1 %fusion.27 = f32[1024,768]{1,0:T(8,128)} fusion(bf16[1024,384]{1,0:T(8,128)(2,1)} %copy-done.1, bf16[3,768,384]{2,1,0:T(8,128)(2,1)} %all-gather.2.cloned.1.call-done), kind=kOutput, calls=%fused_computation.46 | convolution fusion | flops 603979776 | bytes 4521984 | tf_op jit(solution)/shard_map/dot_general | solution.py:36
  136.4 0.0 copy-done.6
  136.4 3.8 %fusion.26 = f32[1024,768]{1,0:T(8,128)} fusion(bf16[1024,384]{1,0:T(8,128)(2,1)S(1)} %bitcast.82, bf16[3,768,384]{2,1,0:T(8,128)(2,1)} %all-gather.2.cloned.1.call-done), kind=kOutput, calls=%fused_computation.45 | convolution fusion | flops 603979776 | bytes 4521984 | tf_op jit(solution)/shard_map/dot_general | solution.py:36
  140.2 71.7 %reduce-scatter.5.cloned.1.call-done = f32[3,96,384]{2,1,0:T(8,128)} async-done(((f32[3,768,384]{2,1,0:T(8,128)}), f32[3,96,384]{2,1,0:T(8,128)}) %reduce-scatter.5.cloned.1.call-update) | async-done | bytes 442384 | tf_op jit(solution)/shard_map/reduce_scatter | solution.py:108
  211.9 2.2 copy.24
  214.1 2.3 reshape.67
  216.3 0.0 reduce-scatter.7.cloned.1.call-update
  216.4 0.0 copy-start.3
  216.4 6.0 %fusion.16 = (f32[1024]{0:T(1024)S(1)}, f32[1024,768]{1,0:T(8,128)S(1)}) fusion(f32[2,512,768]{2,1,0:T(8,128)S(1)} %get-tuple-element.3, bf16[1024,384]{1,0:T(8,128)(2,1)} %bitcast.84, bf16[3,768,384]{2,1,0:T(8,128)(2,1)} %all-gather.2.cloned.1.call-done, f32[1024,768]{1,0:T(8,128)} %fusion.26, f32[1024,768]{1,0:T(8,128)} %fusion.27), kind=kOutput, calls=%fused_computation.25 | convolution fusion | flops 621280256 | bytes 13963264 | tf_op jit(solution)/shard_map/dot_general | solution.py:36
  222.4 0.0 copy-done.3
  222.4 1.9 fusion.15
  224.4 13.8 %reduce-scatter.7.cloned.1.call-done = f32[96,288]{1,0:T(8,128)} async-done(((f32[384,288]{1,0:T(8,128)}), f32[96,288]{1,0:T(8,128)}) %reduce-scatter.7.cloned.1.call-update) | async-done | bytes 110608
  238.1 1.0 reshape.68
  239.2 0.8 copy.25
  (3 shorter events, 0.0 us)
Async XLA Ops:
  7.2 91.4 %all-gather.2.cloned.1.call-start = ((), (), s32[]{:S(2)}) async-start(), calls=%async_computation.2 | async-start | bytes 1990656 | tf_op jit(solution)/shard_map/all_gather | solution.py:66
  17.1 194.8 %reduce-scatter.5.cloned.1.call-start = ((), (), s32[]{:S(2)}) async-start(), calls=%async_computation.3 | async-start | bytes 3981312 | tf_op jit(solution)/shard_map/reduce_scatter | solution.py:108
  17.1 1.9 copy-start
  19.1 10.5 %copy-start.7 = (bf16[96,96]{1,0:T(8,128)(2,1)S(1)}, bf16[96,96]{1,0:T(8,128)(2,1)}, u32[]{:S(2)}) copy-start(bf16[96,96]{1,0:T(8,128)(2,1)} %param.6) | copy-start | bytes 55300
  21.5 77.1 %collective-permute-start.1 = (bf16[2,512,768]{2,1,0:T(8,128)(2,1)}, bf16[2,512,768]{2,1,0:T(8,128)(2,1)}, u32[]{:S(2)}, u32[]{:S(2)}) collective-permute-start(bf16[2,512,768]{2,1,0:T(8,128)(2,1)} %get-tuple-element.2), channel_id=1, source_target_pairs={{2,0},{3,1},{6,4},{7,5},{10,8},{11,9},{14,12},{15,13},{18,16},{19,... | collective-permute-start | bytes 4718600 | tf_op jit(solution)/shard_map/ppermute | solution.py:17
  22.7 78.5 %collective-permute-start = (bf16[2,512,768]{2,1,0:T(8,128)(2,1)}, bf16[2,512,768]{2,1,0:T(8,128)(2,1)}, u32[]{:S(2)}, u32[]{:S(2)}) collective-permute-start(bf16[2,512,768]{2,1,0:T(8,128)(2,1)} %get-tuple-element.2), channel_id=1, source_target_pairs={{0,2},{1,3},{4,6},{5,7},{8,10},{9,11},{12,14},{13,15},{16,18},{17,... | collective-permute-start | bytes 4718600 | tf_op jit(solution)/shard_map/ppermute | solution.py:17
  98.6 2.7 %copy-start.4 = (bf16[3,768,384]{2,1,0:T(8,128)(2,1)S(1)}, bf16[3,768,384]{2,1,0:T(8,128)(2,1)}, u32[]{:S(2)}) copy-start(bf16[3,768,384]{2,1,0:T(8,128)(2,1)} %all-gather.2.cloned.1.call-done) | copy-start | bytes 5308420
  103.6 2.5 %copy-start.2 = (f32[1024,384]{1,0:T(8,128)S(1)}, f32[1024,384]{1,0:T(8,128)}, u32[]{:S(2)}) copy-start(f32[1024,384]{1,0:T(8,128)} %fusion.31) | copy-start | bytes 4718596
  107.4 9.2 %copy-start.1 = (bf16[1024,384]{1,0:T(8,128)(2,1)}, bf16[1024,384]{1,0:T(8,128)(2,1)S(1)}, u32[]{:S(2)}) copy-start(bf16[1024,384]{1,0:T(8,128)(2,1)S(1)} %fusion.25) | copy-start | bytes 2359300
  107.4 16.5 %collective-permute-start.2 = (bf16[2,512,384]{2,1,0:T(8,128)(2,1)S(1)}, bf16[2,512,384]{2,1,0:T(8,128)(2,1)S(1)}, u32[]{:S(2)}, u32[]{:S(2)}) collective-permute-start(bf16[2,512,384]{2,1,0:T(8,128)(2,1)S(1)} %bitcast.77), channel_id=1, source_target_pairs={{2,0},{3,1},{6,4},{7,5},{10,8},{11,9},{14,12},{15,13},{18,16},{19,... | collective-permute-start | bytes 2359304 | tf_op jit(solution)/shard_map/ppermute | solution.py:17
  108.7 18.0 %collective-permute-start.3 = (bf16[2,512,384]{2,1,0:T(8,128)(2,1)S(1)}, bf16[2,512,384]{2,1,0:T(8,128)(2,1)S(1)}, u32[]{:S(2)}, u32[]{:S(2)}) collective-permute-start(bf16[2,512,384]{2,1,0:T(8,128)(2,1)S(1)} %bitcast.78), channel_id=1, source_target_pairs={{0,2},{1,3},{4,6},{5,7},{8,10},{9,11},{12,14},{13,15},{16,18},{17,... | collective-permute-start | bytes 2359304 | tf_op jit(solution)/shard_map/ppermute | solution.py:17
  123.9 2.7 %copy-start.5 = (bf16[2,512,384]{2,1,0:T(8,128)(2,1)}, bf16[2,512,384]{2,1,0:T(8,128)(2,1)S(1)}, u32[]{:S(2)}) copy-start(bf16[2,512,384]{2,1,0:T(8,128)(2,1)S(1)} %collective-permute-done.2) | copy-start | bytes 2359300
  126.7 0.9 copy-start.8
  132.0 106.1 %reduce-scatter.7.cloned.1.call-start = ((), (), s32[]{:S(2)}) async-start(), calls=%async_computation.4 | async-start | bytes 737280
  132.3 4.1 %copy-start.6 = (bf16[2,512,384]{2,1,0:T(8,128)(2,1)S(1)}, bf16[2,512,384]{2,1,0:T(8,128)(2,1)}, u32[]{:S(2)}) copy-start(bf16[2,512,384]{2,1,0:T(8,128)(2,1)} %copy-done.5) | copy-start | bytes 2359300
  216.4 6.1 %copy-start.3 = (bf16[2,512,768]{2,1,0:T(8,128)(2,1)S(1)}, bf16[2,512,768]{2,1,0:T(8,128)(2,1)}, u32[]{:S(2)}) copy-start(bf16[2,512,768]{2,1,0:T(8,128)(2,1)} %param.7) | copy-start | bytes 4718596
Sparse Core Ops, SparseCore 0:
  17.2 46.5 all-gather.1
  132.2 79.6 reduce-scatter.4
  216.5 21.5 reduce-scatter.6
where the time goes:
time: 247 us; the launch traced here: 246 us
  waiting for transfers between devices  92.9 us (38%)
  blocking collectives  73.2 us (30%)
  matrix products  32.5 us (13%)
  starting transfers between devices  15.2 us (6%)
  between operations  14 us (6%)
  other arithmetic  9.51 us (4%)
  local copies, waits for them, and re-layouts  9.25 us (4%)
    reduce_scatter x1, waiting for transfers between devices, body(): lax.psum_scatter(conv_terms, 'dp', scatter_dimension=1, tiled=True)  71.7 us
    all_gather x1, blocking collectives, body(): lax.all_gather(point_weight, 'seq', axis=0, tiled=True)  33.4 us
    all_gather x1, blocking collectives, body(): lax.all_gather(columns[1], 'dp', axis=1, tiled=True)  31.9 us
    dot_general x7, matrix products, product(): return jnp.dot(left, right, preferred_element_type=jnp.float32)  24.9 us
    ppermute x4, starting transfers between devices, from_behind(): return lax.ppermute(x, axis, pairs)  14.9 us
    unnamed x4, waiting for transfers between devices  13.8 us
    unnamed x24, local copies, waits for them, and re-layouts  8.2 us
    all_gather x1, blocking collectives, body(): lax.all_gather(conv_weight, 'seq', axis=2, tiled=True)  7.91 us
  transfers between devices with their start and end apart: 7, of which 3 were waited for; matrix products, arithmetic and copies ran while one was open for 13% of the time, Pallas kernels for 0%

commit v1 on v0

--- a/solution.py
+++ b/solution.py
@@ -1,6 +1,8 @@
 import jax
 import jax.numpy as jnp
 from jax import lax
+from jax.experimental import pallas as pl
+from jax.experimental.pallas import tpu as pltpu
 from jax.sharding import PartitionSpec as P
 
 SPAN = 2
@@ -109,10 +111,325 @@
     conv_grad = lax.psum_scatter(partial_terms, "seq", scatter_dimension=2, tiled=True)
     return (input_grad, conv_grad)
 
+MESH = pl.DeviceIdType.MESH
+ZS, YS = 4, 2
+ORDER = (1, 3, 2)
+
+
+def fits(mesh):
+    return mesh.shape["dp"] == ZS * YS and mesh.shape["seq"] == 2 * SPAN
+
+
+def fused_kernel(
+    grad_scale,
+    x_ref, w_ref, cot_ref,
+    out_ref, conv_ref,
+    planes, w_halo, w_mid, w_point,
+    acted, normed, slope, scale,
+    mid, inner, tap_out, tap_in, pre_out, pre_in,
+    g_halo, g_mid, own, sib_out, sib_in, y_out, y_in, z_out, z_in, last, x_out, x_in,
+    z_s, z_r, yw_s, yw_r, xw_s, xw_r, dx_s, dx_r, dy_s, dy_r, sb_s, sb_r,
+    tp_s, tp_r, gp_s, gp_r, cs_s, cs_r, cy_s, cy_r, cz_s, cz_r, cx_s, cx_r,
+):
+    rows, width = x_ref.shape
+    hidden = mid.shape[1]
+    part = w_ref.shape[0]
+    half = part // 2
+    lane = hidden // 4
+    d = lax.axis_index("dp")
+    s = lax.axis_index("seq")
+    z, y = lax.div(d, YS), lax.rem(d, YS)
+    x, c = lax.div(s, 2), lax.rem(s, 2)
+    s_x = (1 - x) * 2 + c
+    s_c = x * 2 + 1 - c
+    d_y = z * YS + 1 - y
+    sib, xn, yn = (d, s_c), (d, s_x), (d_y, s)
+
+    def zdev(k):
+        return (lax.rem(z + k, ZS) * YS + y, s)
+
+    barrier = pltpu.get_barrier_semaphore()
+    for dev in (sib, xn, yn, zdev(1), zdev(2), zdev(3)):
+        pl.semaphore_signal(barrier, inc=1, device_id=dev, device_id_type=MESH)
+
+    def remote(src, dst, ssem, rsem, dev):
+        return pltpu.make_async_remote_copy(
+            src_ref=src, dst_ref=dst, send_sem=ssem, recv_sem=rsem,
+            device_id=dev, device_id_type=MESH)
+
+    def piece(plane, dd, start=0, size=part):
+        return planes.at[plane, pl.ds(pl.multiple_of(dd * part + start, 16), size), :]
+
+    pending = []
+
+    def send(src, dst, ssem, rsem, dev):
+        copy = remote(src, dst, ssem, rsem, dev)
+        copy.start()
+        pending.append(copy)
+
+    def arrived(ref, ssem, rsem, dev):
+        remote(ref, ref, ssem, rsem, dev).wait_recv()
+
+    def from_k(k, yy):
+        return lax.rem(z + ZS - k, ZS) * YS + yy
+
+    planes[s, pl.ds(pl.multiple_of(d * part, 16), part), :] = w_ref[...]
+    pl.semaphore_wait(barrier, 6)
+
+    def to_sib(plane, dd, n):
+        ref = piece(plane, dd)
+        send(ref, ref, sb_s.at[n], sb_r.at[n], sib)
+
+    def spread(k):
+        ref = piece(s, from_k(k, y))
+        send(ref, ref, xw_s.at[k], xw_r.at[k], xn)
+        send(ref, ref, yw_s.at[k], yw_r.at[k], yn)
+        to_sib(s, from_k(k, y), k)
+
+    for k in ORDER:
+        ref = piece(s, d)
+        send(ref, ref, z_s.at[k], z_r.at[k], zdev(k))
+    spread(0)
+
+    step = 32
+    quarter = rows // 8
+
+    def activations(q):
+        def one(i, carry):
+            at = pl.ds(pl.multiple_of(q * quarter + i * step, 16), step)
+            v = x_ref[at, :].astype(jnp.float32)
+            r = lax.rsqrt(jnp.mean(v * v, axis=-1, keepdims=True) + EPSILON)
+            n = v * r
+            n2 = n * n
+            t = jnp.tanh(GELU_SCALE * (n + GELU_CUBIC * n2 * n))
+            normed[at, :] = n
+            acted[at, :] = (0.5 * n * (1.0 + t)).astype(jnp.bfloat16)
+            slope[at, :] = 0.5 * (1.0 + t) + 0.5 * n * (1.0 - t * t) * GELU_SCALE * (
+                1.0 + 3.0 * GELU_CUBIC * n2)
+            scale[at, :] = jnp.broadcast_to(r, (step, 128))
+            return carry
+        lax.fori_loop(0, quarter // step, one, 0)
+
+    def take_y(k):
+        dd = from_k(k, 1 - y)
+        arrived(piece(s, dd), yw_s.at[k], yw_r.at[k], yn)
+        ref = piece(s, dd, 0, half)
+        send(ref, ref, dx_s.at[k], dx_r.at[k], xn)
+        to_sib(s, dd, 4 + k)
+
+    def take_x(k):
+        dd = from_k(k, y)
+        arrived(piece(s_x, dd), xw_s.at[k], xw_r.at[k], xn)
+        ref = piece(s_x, dd, half, half)
+        send(ref, ref, dy_s.at[k], dy_r.at[k], yn)
+        to_sib(s_x, dd, 8 + k)
+
+    def take_diagonal(k):
+        dd = from_k(k, 1 - y)
+        arrived(piece(s_x, dd, 0, half), dx_s.at[k], dx_r.at[k], xn)
+        arrived(piece(s_x, dd, half, half), dy_s.at[k], dy_r.at[k], yn)
+        to_sib(s_x, dd, 12 + k)
+
+    activations(0)
+    activations(1)
+    for n, k in enumerate(ORDER):
+        arrived(piece(s, from_k(k, y)), z_s.at[k], z_r.at[k], zdev(k))
+        spread(k)
+        take_y(((0,) + ORDER)[n])
+        take_x(((0,) + ORDER)[n])
+        activations(2 + 2 * n)
+        activations(3 + 2 * n)
+    take_y(ORDER[2])
+    take_x(ORDER[2])
+    for k in (0,) + ORDER:
+        take_diagonal(k)
+    for plane, yy, n in ((s_c, y, 0), (s_c, 1 - y, 4), ((1 - x) * 2 + 1 - c, y, 8),
+                         ((1 - x) * 2 + 1 - c, 1 - y, 12)):
+        for k in range(ZS):
+            arrived(piece(plane, from_k(k, yy)), sb_s.at[n + k], sb_r.at[n + k], sib)
+
+    block = 128
+    is_low = x == 0
+
+    def assemble(i, carry):
+        at = pl.ds(pl.multiple_of(i * block, 16), block)
+        got = [planes[p, at, :] for p in range(4)]
+
+        def columns(m):
+            return jnp.concatenate([g[:, m * lane:(m + 1) * lane] for g in got], axis=1)
+
+        w_halo[at, :] = jnp.where(is_low, columns(0), columns(2))
+        w_mid[at, :] = columns(1)
+        w_point[at, :] = columns(3)
+        return carry
+
+    lax.fori_loop(0, width // block, assemble, 0)
+
+    chunks = 4
+    size = rows // chunks
+
+    def chunk(q):
+        return pl.ds(q * size, size)
+
+    for q in range(chunks):
+        tap_out[chunk(q), :] = product(acted[chunk(q), :], w_halo[...]).astype(jnp.bfloat16)
+        send(tap_out.at[chunk(q)], tap_in.at[chunk(q)], tp_s.at[q], tp_r.at[q], xn)
+
+    for q in range(chunks):
+        mid[chunk(q), :] = product(acted[chunk(q), :], w_mid[...])
+        inner[chunk(q), :] = product(cot_ref[chunk(q), :], w_point[...])
+
+    for q in range(chunks):
+        arrived(tap_in.at[chunk(q)], tp_s.at[q], tp_r.at[q], xn)
+
+        def one(i, carry):
+            at = pl.ds(pl.multiple_of(q * size + i * step, 16), step)
+            pre = mid[at, :] + tap_in[at, :].astype(jnp.float32)
+            pre_out[at, :] = (inner[at, :] * gelu_slope(pre)).astype(jnp.bfloat16)
+            return carry
+
+        lax.fori_loop(0, size // step, one, 0)
+        send(pre_out.at[chunk(q)], pre_in.at[chunk(q)], gp_s.at[q], gp_r.at[q], xn)
+
+    over_rows = (((0,), (0,)), ((), ()))
+    over_lanes = (((1,), (1,)), ((), ()))
+
+    def outer(a, b):
+        return lax.dot_general(a, b, over_rows, preferred_element_type=jnp.float32)
+
+    def back(a, b):
+        return lax.dot_general(a, b, over_lanes, preferred_element_type=jnp.float32)
+
+    g_mid[...] = outer(acted[...], pre_out[...])
+
+    for q in range(chunks):
+        arrived(pre_in.at[chunk(q)], gp_s.at[q], gp_r.at[q], xn)
+    g_halo[...] = outer(acted[...], pre_in[...])
+
+    def pack(i, carry):
+        at = pl.ds(pl.multiple_of(i * 64, 16), 64)
+        a, b = g_halo[at, :] * grad_scale, g_mid[at, :] * grad_scale
+
+        def columns(core):
+            return jnp.concatenate(
+                [g[:, p * lane:(p + 1) * lane] for g in (a, b) for p in (core, 2 + core)], axis=1)
+
+        even, odd = columns(0), columns(1)
+        first = c == 0
+        own[at, :] = jnp.where(first, even, odd)
+        sib_out[at, :] = jnp.where(first, odd, even).astype(jnp.bfloat16)
+        return carry
+
+    lax.fori_loop(0, width // 64, pack, 0)
+    send(sib_out, sib_in, cs_s.at[0], cs_r.at[0], sib)
+
+    def finish(q):
+        act = back(pre_in[chunk(q), :], w_halo[...]) + back(pre_out[chunk(q), :], w_mid[...])
+        mark = pl.ds(q * size, size)
+        slope[mark, :] = act * slope[mark, :]
+
+        def one(i, carry):
+            at = pl.ds(pl.multiple_of(q * size + i * step, 16), step)
+            g, n = slope[at, :], normed[at, :]
+            center = jnp.mean(g * n, axis=-1, keepdims=True)
+            r = scale[at, :][:, :1]
+            out_ref[at, :] = (cot_ref[at, :].astype(jnp.float32) + r * (g - n * center)).astype(
+                jnp.bfloat16)
+            return carry
+
+        lax.fori_loop(0, size // step, one, 0)
+
+    def dest(k, yy):
+        return pl.ds(pl.multiple_of((lax.rem(z + k, ZS) * YS + yy) * part, 16), part)
+
+    arrived(sib_in, cs_s.at[0], cs_r.at[0], sib)
+    for k in ORDER + (0,):
+        at = dest(k, 1 - y)
+        y_out[k] = (own[at, :] + sib_in[at, :].astype(jnp.float32)).astype(jnp.bfloat16)
+        send(y_out.at[k], y_in.at[k], cy_s.at[k], cy_r.at[k], yn)
+    finish(0)
+    for n, k in enumerate(ORDER + (0,)):
+        at = dest(k, y)
+        arrived(y_in.at[k], cy_s.at[k], cy_r.at[k], yn)
+        total = own[at, :] + sib_in[at, :].astype(jnp.float32) + y_in[k].astype(jnp.float32)
+        if k:
+            z_out[k] = total.astype(jnp.bfloat16)
+            send(z_out.at[k], z_in.at[k], cz_s.at[k], cz_r.at[k], zdev(k))
+        else:
+            last[...] = total
+    finish(1)
+    finish(2)
+    for k in ORDER:
+        arrived(z_in.at[k], cz_s.at[k], cz_r.at[k], zdev(k))
+    last[...] = last[...] + (z_in[1].astype(jnp.float32) + z_in[2].astype(jnp.float32)
+                             + z_in[3].astype(jnp.float32))
+    x_out[...] = last[...].astype(jnp.bfloat16)
+    send(x_out, x_in, cx_s.at[0], cx_r.at[0], xn)
+    finish(3)
+    arrived(x_in, cx_s.at[0], cx_r.at[0], xn)
+    mine, theirs = last[...], x_in[...].astype(jnp.float32)
+
+    def pick(v, slot):
+        low = v[:, (2 * slot) * lane:(2 * slot + 1) * lane]
+        high = v[:, (2 * slot + 1) * lane:(2 * slot + 2) * lane]
+        return jnp.where(is_low, low, high)
+
+    own_halo, their_halo = pick(mine, 0), pick(theirs, 0)
+    conv_ref[0] = jnp.where(is_low, own_halo, their_halo)
+    conv_ref[1] = pick(mine, 1) + pick(theirs, 1)
+    conv_ref[2] = jnp.where(is_low, their_halo, own_halo)
+    for copy in pending:
+        copy.wait_send()
+
+
+def fused_body(inputs, conv_weight, point_weight, cotangent):
+    samp_count, bin_count, width = inputs.shape
+    rows = samp_count * bin_count
+    part = conv_weight.shape[1]
+    hidden = conv_weight.shape[2] * lax.axis_size("seq")
+    grad_scale = float(rows * lax.axis_size("dp") * lax.axis_size("seq")) ** (-0.5)
+    packed = jnp.concatenate([conv_weight[0], conv_weight[1], conv_weight[2], point_weight.T], axis=1)
+    bf, f32 = jnp.bfloat16, jnp.float32
+
+    def vmem(kind, *dims):
+        return pltpu.VMEM(dims, kind)
+
+    def sems(n):
+        return [pltpu.SemaphoreType.DMA((n,))] * 2
+
+    whole = pl.BlockSpec(memory_space=pltpu.VMEM)
+    grad, conv_grad = pl.pallas_call(
+        lambda *refs: fused_kernel(grad_scale, *refs),
+        out_shape=(
+            jax.ShapeDtypeStruct((rows, width), bf),
+            jax.ShapeDtypeStruct(conv_weight.shape, f32),
+        ),
+        in_specs=[whole] * 3,
+        out_specs=(whole, whole),
+        scratch_shapes=[
+            vmem(bf, 4, width, hidden), vmem(bf, width, hidden), vmem(bf, width, hidden),
+            vmem(bf, width, hidden),
+            vmem(bf, rows, width), vmem(f32, rows, width), vmem(f32, rows, width),
+            vmem(f32, rows, 128),
+            vmem(f32, rows, hidden), vmem(f32, rows, hidden), vmem(bf, rows, hidden),
+            vmem(bf, rows, hidden), vmem(bf, rows, hidden), vmem(bf, rows, hidden),
+            vmem(f32, width, hidden), vmem(f32, width, hidden), vmem(f32, width, hidden),
+            vmem(bf, width, hidden), vmem(bf, width, hidden),
+            vmem(bf, 4, part, hidden), vmem(bf, 4, part, hidden),
+            vmem(bf, 4, part, hidden), vmem(bf, 4, part, hidden),
+            vmem(f32, part, hidden), vmem(bf, part, hidden), vmem(bf, part, hidden),
+            *sems(4), *sems(4), *sems(4), *sems(4), *sems(4), *sems(16),
+            *sems(4), *sems(4), *sems(1), *sems(4), *sems(4), *sems(1),
+        ],
+        compiler_params=pltpu.CompilerParams(
+            collective_id=0, has_side_effects=True, vmem_limit_bytes=56 * 1024 * 1024),
+    )(inputs.reshape(rows, width), packed, cotangent.reshape(rows, width))
+    return grad.reshape(samp_count, bin_count, width), conv_grad
+
 
 def solution(mesh):
     return jax.shard_map(
-        body,
+        fused_body if fits(mesh) else body,
         mesh=mesh,
         in_specs=(P("dp", "seq", None), P(None, "dp", "seq"), P("seq", "dp"), P("dp", "seq", None)),
         out_specs=(P("dp", "seq", None), P(None, "dp", "seq")),

time: 247 us -> 90.6 us (0.37)
  waiting for transfers between devices: 92.9 us -> 0 us
  Pallas kernels: 0 us -> 84 us
  blocking collectives: 73.2 us -> 0 us
  matrix products: 32.5 us -> 0 us
  starting transfers between devices: 15.2 us -> 0 us
  between operations: 14 us -> 0.65 us
  other arithmetic: 9.51 us -> 0.74 us
  local copies, waits for them, and re-layouts: 9.25 us -> 4.97 us
    pallas_call x0 -> x1, Pallas kernels: none -> 84 us  [fused_body(): pl.pallas_call(lambda *refs: fused_kernel(grad_scale, *refs), out_shape=(...]
    all_gather x3 -> x0, blocking collectives: 73.2 us -> none  [the longest x1 33.4 us: body(): lax.all_gather(point_weight, 'seq', axis=0, tiled=True)]
    reduce_scatter x1 -> x0, waiting for transfers between devices: 71.7 us -> none  [body(): lax.psum_scatter(conv_terms, 'dp', scatter_dimension=1, tiled=True)]
    dot_general x10 -> x0, matrix products: 32.5 us -> none  [the longest x7 24.9 us: product(): return jnp.dot(left, right, preferred_element_type=jnp.float32)]
    ppermute x4 -> x0, starting transfers between devices: 14.9 us -> none  [from_behind(): return lax.ppermute(x, axis, pairs)]
    unnamed x4 -> x0, waiting for transfers between devices: 13.8 us -> none
    ppermute x4 -> x0, waiting for transfers between devices: 7.37 us -> none  [from_behind(): return lax.ppermute(x, axis, pairs)]
    convert_element_type x3 -> x0, other arithmetic: 5.53 us -> none  [the longest x1 2.38 us: body(): acted = gelu_tanh(normed).astype(jnp.bfloat16)]
  transfers between devices with their start and end apart: 7 -> 0, of which waited for: 3 -> 0; matrix products, arithmetic and copies ran while one was open for 13% -> 0% of each run, Pallas kernels for 0% -> 0%
where the time goes in v1:
time: 90.6 us; the launch traced here: 90.4 us
  Pallas kernels  84 us (93%)
  local copies, waits for them, and re-layouts  4.97 us (5%)
    pallas_call x1, Pallas kernels, fused_body(): pl.pallas_call(lambda *refs: fused_kernel(grad_scale, *refs), out_shape=(...  84 us
    unnamed x5, local copies, waits for them, and re-layouts  4.18 us

profile of v1, /device:TPU:0, one launch (start us, length us, event | category | flops | bytes accessed | tf_op | source)
XLA Modules:
  0.0 90.4 jit_solution(8821012195316766570)
XLA Ops:
  0.6 0.8 copy.6
  1.5 0.8 slice_bitcast_fusion.2
  2.3 0.7 pad_maximum_fusion.refs_1_
  3.0 84.0 %shard_map.59 = (bf16[1024,768]{1,0:T(8,128)(2,1)}, f32[3,96,96]{2,1,0:T(8,128)}) custom-call(bf16[1024,768]{1,0:T(8,128)(2,1)} %bitcast.10, bf16[96,384]{1,0:T(8,128)(2,1)} %pad_maximum_fusion.refs_1_, bf16[1024,768]{1,0:T(8,128)(2,1)} %bitcast.11), custom_call_target="tpu_custom_call" | custom-call | tf_op jit(solution)/shard_map/pallas_call | solution.py:401
  87.0 0.0 copy-start
  87.0 2.7 %copy.9 = bf16[2,512,768]{2,1,0:T(8,128)(2,1)} copy(bf16[2,512,768]{2,1,0:T(8,128)(2,1)} %bitcast.12) | data formatting | bytes 3145728
  89.7 0.0 copy-done
  89.7 0.7 copy.10
Async XLA Ops:
  87.0 2.7 %copy-start = (f32[3,96,96]{2,1,0:T(8,128)S(1)}, f32[3,96,96]{2,1,0:T(8,128)}, u32[]{:S(2)}) copy-start(f32[3,96,96]{2,1,0:T(8,128)} %get-tuple-element.12) | copy-start | bytes 331780

commit v2 on v0

--- a/solution.py
+++ b/solution.py
@@ -1,6 +1,8 @@
 import jax
 import jax.numpy as jnp
 from jax import lax
+from jax.experimental import pallas as pl
+from jax.experimental.pallas import tpu as pltpu
 from jax.sharding import PartitionSpec as P
 
 SPAN = 2
@@ -109,10 +111,362 @@
     conv_grad = lax.psum_scatter(partial_terms, "seq", scatter_dimension=2, tiled=True)
     return (input_grad, conv_grad)
 
+MESH = pl.DeviceIdType.MESH
+ZS, YS = 4, 2
+ORDER = (1, 3, 2)
+
+
+def fits(mesh):
+    return mesh.shape["dp"] == ZS * YS and mesh.shape["seq"] == 2 * SPAN
+
+
+def fused_kernel(
+    grad_scale,
+    x_ref, conv_w_ref, point_w_ref, cot_ref,
+    out_ref, conv_ref,
+    w_own, w_in, first_w, rest_w, w_halo, w_mid, w_point,
+    acted, normed, slope, scale,
+    mid, inner, tap_out, tap_in, pre_out, pre_in,
+    grads, own, sib_out, sib_in, y_out, y_in, z_out, z_in, last, x_out, x_in,
+    wx_s, wx_r, wz_s, wz_r, wy_s, wy_r, wc_s, wc_r,
+    tp_s, tp_r, gp_s, gp_r, cs_s, cs_r, cy_s, cy_r, cz_s, cz_r, cx_s, cx_r,
+):
+    rows, width = x_ref.shape
+    hidden = mid.shape[1]
+    part = w_own.shape[0]
+    lane = hidden // 4
+    d = lax.axis_index("dp")
+    s = lax.axis_index("seq")
+    z, y = lax.div(d, YS), lax.rem(d, YS)
+    x, c = lax.div(s, 2), lax.rem(s, 2)
+    is_low = x == 0
+    sib = (d, x * 2 + 1 - c)
+    xn = (d, (1 - x) * 2 + c)
+    yn = (z * YS + 1 - y, s)
+
+    def zdev(k):
+        return (lax.rem(z + k, ZS) * YS + y, s)
+
+    barrier = pltpu.get_barrier_semaphore()
+    for dev in (sib, xn, yn, zdev(1), zdev(2), zdev(3)):
+        pl.semaphore_signal(barrier, inc=1, device_id=dev, device_id_type=MESH)
+
+    def remote(src, dst, ssem, rsem, dev):
+        return pltpu.make_async_remote_copy(
+            src_ref=src, dst_ref=dst, send_sem=ssem, recv_sem=rsem,
+            device_id=dev, device_id_type=MESH)
+
+    pending = []
+
+    def send(src, dst, ssem, rsem, dev):
+        copy = remote(src, dst, ssem, rsem, dev)
+        copy.start()
+        pending.append(copy)
+
+    def arrived(ref, ssem, rsem, dev):
+        remote(ref, ref, ssem, rsem, dev).wait_recv()
+
+    def from_k(k, yy):
+        return lax.rem(z + ZS - k, ZS) * YS + yy
+
+    step = 32
+    eighth = rows // 8
+
+    def activations(q):
+        def one(i, carry):
+            at = pl.ds(pl.multiple_of(q * eighth + i * step, 16), step)
+            v = x_ref[at, :].astype(jnp.float32)
+            r = lax.rsqrt(jnp.mean(v * v, axis=-1, keepdims=True) + EPSILON)
+            n = v * r
+            n2 = n * n
+            t = jnp.tanh(GELU_SCALE * (n + GELU_CUBIC * n2 * n))
+            normed[at, :] = n
+            acted[at, :] = (0.5 * n * (1.0 + t)).astype(jnp.bfloat16)
+            slope[at, :] = 0.5 * (1.0 + t) + 0.5 * n * (1.0 - t * t) * GELU_SCALE * (
+                1.0 + 3.0 * GELU_CUBIC * n2)
+            scale[at, :] = jnp.broadcast_to(r, (step, 128))
+            return carry
+        lax.fori_loop(0, eighth // step, one, 0)
+
+    w_own[...] = jnp.concatenate(
+        [conv_w_ref[0], conv_w_ref[2], conv_w_ref[1],
+         point_w_ref[...].astype(jnp.float32).T.astype(jnp.bfloat16)], axis=1)
+    pl.semaphore_wait(barrier, 6)
+    send(w_own, w_in, wx_s.at[0], wx_r.at[0], xn)
+    activations(0)
+    activations(1)
+    arrived(w_in, wx_s.at[0], wx_r.at[0], xn)
+
+    mine, theirs = w_own[...], w_in[...]
+    low, high = jnp.where(is_low, mine, theirs), jnp.where(is_low, theirs, mine)
+
+    def live(v):
+        return jnp.where(is_low, v[:, :lane], v[:, lane:2 * lane])
+
+    at_own = pl.ds(pl.multiple_of(d * part, 16), part)
+    first_w[c, at_own, :] = jnp.concatenate(
+        [live(low), live(high), jnp.zeros((part, 256 - 2 * lane), jnp.bfloat16)], axis=1)
+    rest_w[c, at_own, :] = jnp.concatenate([low[:, 2 * lane:], high[:, 2 * lane:]], axis=1)
+
+    bufs = (first_w, rest_w)
+
+    def piece(p, core, dd):
+        return bufs[p].at[core, pl.ds(pl.multiple_of(dd * part, 16), part), :]
+
+    def forward(p, k):
+        ref = piece(p, c, from_k(k, y))
+        send(ref, ref, wy_s.at[p, k], wy_r.at[p, k], yn)
+        send(ref, ref, wc_s.at[p, k], wc_r.at[p, k], sib)
+
+    def begin(p):
+        ref = piece(p, c, d)
+        for k in ORDER:
+            send(ref, ref, wz_s.at[p, k], wz_r.at[p, k], zdev(k))
+        forward(p, 0)
+
+    def take_z(p, k):
+        arrived(piece(p, c, from_k(k, y)), wz_s.at[p, k], wz_r.at[p, k], zdev(k))
+        forward(p, k)
+
+    def take_y(p, k):
+        ref = piece(p, c, from_k(k, 1 - y))
+        arrived(ref, wy_s.at[p, k], wy_r.at[p, k], yn)
+        send(ref, ref, wc_s.at[p, 4 + k], wc_r.at[p, 4 + k], sib)
+
+    def take_core(p):
+        for n, yy in ((0, y), (4, 1 - y)):
+            for k in range(ZS):
+                arrived(piece(p, 1 - c, from_k(k, yy)), wc_s.at[p, n + k], wc_r.at[p, n + k], sib)
+
+    begin(0)
+    activations(2)
+    for n, k in enumerate(ORDER):
+        take_z(0, k)
+        activations(3 + n)
+    begin(1)
+    for n, k in enumerate((0,) + ORDER):
+        take_y(0, k)
+        if n < 2:
+            activations(6 + n)
+    take_core(0)
+
+    block = 128
+
+    def assemble_first(i, carry):
+        at = pl.ds(pl.multiple_of(i * block, 16), block)
+        even, odd = first_w[0, at, :], first_w[1, at, :]
+        w_halo[at, :] = jnp.concatenate(
+            [even[:, :lane], odd[:, :lane], even[:, lane:2 * lane], odd[:, lane:2 * lane]], axis=1)
+        return carry
+
+    lax.fori_loop(0, width // block, assemble_first, 0)
+
+    chunks = 4
+    size = rows // chunks
+
+    def chunk(q):
+        return pl.ds(q * size, size)
+
+    def tap(q):
+        tap_out[chunk(q), :] = product(acted[chunk(q), :], w_halo[...]).astype(jnp.bfloat16)
+        send(tap_out.at[chunk(q)], tap_in.at[chunk(q)], tp_s.at[q], tp_r.at[q], xn)
+
+    tap(0)
+    for k in ORDER:
+        take_z(1, k)
+    for q in range(1, chunks):
+        tap(q)
+    for k in (0,) + ORDER:
+        take_y(1, k)
+    take_core(1)
+
+    def assemble_rest(i, carry):
+        at = pl.ds(pl.multiple_of(i * block, 16), block)
+        even, odd = rest_w[0, at, :], rest_w[1, at, :]
+
+        def columns(m):
+            return jnp.concatenate(
+                [v[:, p * lane:(p + 1) * lane] for p in (m, 2 + m) for v in (even, odd)], axis=1)
+
+        w_mid[at, :] = columns(0)
+        w_point[at, :] = columns(1)
+        return carry
+
+    lax.fori_loop(0, width // block, assemble_rest, 0)
+
+    for q in range(chunks):
+        mid[chunk(q), :] = product(acted[chunk(q), :], w_mid[...])
+        inner[chunk(q), :] = product(cot_ref[chunk(q), :], w_point[...])
+
+    for q in range(chunks):
+        arrived(tap_in.at[chunk(q)], tp_s.at[q], tp_r.at[q], xn)
+
+        def one(i, carry):
+            at = pl.ds(pl.multiple_of(q * size + i * step, 16), step)
+            pre = mid[at, :] + tap_in[at, :].astype(jnp.float32)
+            pre_out[at, :] = (inner[at, :] * gelu_slope(pre)).astype(jnp.bfloat16)
+            return carry
+
+        lax.fori_loop(0, size // step, one, 0)
+        send(pre_out.at[chunk(q)], pre_in.at[chunk(q)], gp_s.at[q], gp_r.at[q], xn)
+
+    over_rows = (((0,), (0,)), ((), ()))
+    over_lanes = (((1,), (1,)), ((), ()))
+
+    def outer(a, b):
+        return lax.dot_general(a, b, over_rows, preferred_element_type=jnp.float32)
+
+    def back(a, b):
+        return lax.dot_general(a, b, over_lanes, preferred_element_type=jnp.float32)
+
+    def share_core(t):
+        def pack(i, carry):
+            at = pl.ds(pl.multiple_of(i * 64, 16), 64)
+            g = grads[t, at, :] * grad_scale
+            blank = jnp.zeros((64, 256 - 2 * lane), jnp.float32)
+
+            def columns(core):
+                return jnp.concatenate(
+                    [g[:, p * lane:(p + 1) * lane] for p in (core, 2 + core)] + [blank], axis=1)
+
+            even, odd = columns(0), columns(1)
+            own[t, at, :] = jnp.where(c == 0, even, odd)
+            sib_out[t, at, :] = jnp.where(c == 0, odd, even).astype(jnp.bfloat16)
+            return carry
+
+        lax.fori_loop(0, width // 64, pack, 0)
+        send(sib_out.at[t], sib_in.at[t], cs_s.at[t], cs_r.at[t], sib)
+
+    def dest(k, yy):
+        return pl.ds(pl.multiple_of((lax.rem(z + k, ZS) * YS + yy) * part, 16), part)
+
+    def share_y(t):
+        arrived(sib_in.at[t], cs_s.at[t], cs_r.at[t], sib)
+        for k in ORDER + (0,):
+            at = dest(k, 1 - y)
+            y_out[t, k] = (own[t, at, :] + sib_in[t, at, :].astype(jnp.float32)).astype(jnp.bfloat16)
+            send(y_out.at[t, k], y_in.at[t, k], cy_s.at[t, k], cy_r.at[t, k], yn)
+
+    def share_z(t):
+        for k in ORDER + (0,):
+            at = dest(k, y)
+            arrived(y_in.at[t, k], cy_s.at[t, k], cy_r.at[t, k], yn)
+            total = (own[t, at, :] + sib_in[t, at, :].astype(jnp.float32)
+                     + y_in[t, k].astype(jnp.float32))
+            if k:
+                z_out[t, k] = total.astype(jnp.bfloat16)
+                send(z_out.at[t, k], z_in.at[t, k], cz_s.at[t, k], cz_r.at[t, k], zdev(k))
+            else:
+                last[t] = total
+
+    def share_x(t):
+        for k in ORDER:
+            arrived(z_in.at[t, k], cz_s.at[t, k], cz_r.at[t, k], zdev(k))
+        total = last[t] + (z_in[t, 1].astype(jnp.float32) + z_in[t, 2].astype(jnp.float32)
+                           + z_in[t, 3].astype(jnp.float32))
+        last[t] = total
+        x_out[t] = total.astype(jnp.bfloat16)
+        send(x_out.at[t], x_in.at[t], cx_s.at[t], cx_r.at[t], xn)
+
+    def finish(q):
+        act = back(pre_in[chunk(q), :], w_halo[...]) + back(pre_out[chunk(q), :], w_mid[...])
+        slope[chunk(q), :] = act * slope[chunk(q), :]
+
+        def one(i, carry):
+            at = pl.ds(pl.multiple_of(q * size + i * step, 16), step)
+            g, n = slope[at, :], normed[at, :]
+            center = jnp.mean(g * n, axis=-1, keepdims=True)
+            r = scale[at, :][:, :1]
+            out_ref[at, :] = (cot_ref[at, :].astype(jnp.float32) + r * (g - n * center)).astype(
+                jnp.bfloat16)
+            return carry
+
+        lax.fori_loop(0, size // step, one, 0)
+
+    def halo_term(q):
+        arrived(pre_in.at[chunk(q)], gp_s.at[q], gp_r.at[q], xn)
+        term = outer(acted[chunk(q), :], pre_in[chunk(q), :])
+        grads[0] = term if q == 0 else grads[0] + term
+
+    grads[1] = outer(acted[...], pre_out[...])
+    share_core(1)
+    share_y(1)
+    halo_term(0)
+    share_z(1)
+    finish(0)
+    halo_term(1)
+    share_x(1)
+    finish(1)
+    halo_term(2)
+    halo_term(3)
+    share_core(0)
+    share_y(0)
+    share_z(0)
+    finish(2)
+    share_x(0)
+    finish(3)
+
+    def pick(v):
+        return jnp.where(is_low, v[:, :lane], v[:, lane:2 * lane])
+
+    arrived(x_in.at[1], cx_s.at[1], cx_r.at[1], xn)
+    conv_ref[1] = pick(last[1]) + pick(x_in[1].astype(jnp.float32))
+    arrived(x_in.at[0], cx_s.at[0], cx_r.at[0], xn)
+    own_halo, their_halo = pick(last[0]), pick(x_in[0].astype(jnp.float32))
+    conv_ref[0] = jnp.where(is_low, own_halo, their_halo)
+    conv_ref[2] = jnp.where(is_low, their_halo, own_halo)
+    for copy in pending:
+        copy.wait_send()
+
+
+def fused_body(inputs, conv_weight, point_weight, cotangent):
+    samp_count, bin_count, width = inputs.shape
+    rows = samp_count * bin_count
+    part = conv_weight.shape[1]
+    hidden = conv_weight.shape[2] * lax.axis_size("seq")
+    grad_scale = float(rows * lax.axis_size("dp") * lax.axis_size("seq")) ** (-0.5)
+    bf, f32 = jnp.bfloat16, jnp.float32
+
+    def vmem(kind, *dims):
+        return pltpu.VMEM(dims, kind)
+
+    def sems(*n):
+        return [pltpu.SemaphoreType.DMA(n)] * 2
+
+    whole = pl.BlockSpec(memory_space=pltpu.VMEM)
+    grad, conv_grad = pl.pallas_call(
+        lambda *refs: fused_kernel(grad_scale, *refs),
+        out_shape=(
+            jax.ShapeDtypeStruct((rows, width), bf),
+            jax.ShapeDtypeStruct(conv_weight.shape, f32),
+        ),
+        in_specs=[whole] * 4,
+        out_specs=(whole, whole),
+        scratch_shapes=[
+            vmem(bf, part, hidden), vmem(bf, part, hidden),
+            vmem(bf, 2, width, 256), vmem(bf, 2, width, hidden),
+            vmem(bf, width, hidden), vmem(bf, width, hidden), vmem(bf, width, hidden),
+            vmem(bf, rows, width), vmem(f32, rows, width), vmem(f32, rows, width),
+            vmem(f32, rows, 128),
+            vmem(f32, rows, hidden), vmem(f32, rows, hidden), vmem(bf, rows, hidden),
+            vmem(bf, rows, hidden), vmem(bf, rows, hidden), vmem(bf, rows, hidden),
+            vmem(f32, 2, width, hidden), vmem(f32, 2, width, 256),
+            vmem(bf, 2, width, 256), vmem(bf, 2, width, 256),
+            vmem(bf, 2, 4, part, 256), vmem(bf, 2, 4, part, 256),
+            vmem(bf, 2, 4, part, 256), vmem(bf, 2, 4, part, 256),
+            vmem(f32, 2, part, 256), vmem(bf, 2, part, 256), vmem(bf, 2, part, 256),
+            *sems(1), *sems(2, 4), *sems(2, 4), *sems(2, 8),
+            *sems(4), *sems(4), *sems(2), *sems(2, 4), *sems(2, 4), *sems(2),
+        ],
+        compiler_params=pltpu.CompilerParams(
+            collective_id=0, has_side_effects=True, vmem_limit_bytes=56 * 1024 * 1024),
+    )(inputs.reshape(rows, width), conv_weight, point_weight, cotangent.reshape(rows, width))
+    return grad.reshape(samp_count, bin_count, width), conv_grad
+
 
 def solution(mesh):
     return jax.shard_map(
-        body,
+        fused_body if fits(mesh) else body,
         mesh=mesh,
         in_specs=(P("dp", "seq", None), P(None, "dp", "seq"), P("seq", "dp"), P("dp", "seq", None)),
         out_specs=(P("dp", "seq", None), P(None, "dp", "seq")),

time: 247 us -> 78.3 us (0.32)
  waiting for transfers between devices: 92.9 us -> 0 us
  Pallas kernels: 0 us -> 74.1 us
  blocking collectives: 73.2 us -> 0 us
  matrix products: 32.5 us -> 0 us
  starting transfers between devices: 15.2 us -> 0 us
  between operations: 14 us -> 0.65 us
  other arithmetic: 9.51 us -> 0 us
  local copies, waits for them, and re-layouts: 9.25 us -> 3.35 us
    pallas_call x0 -> x1, Pallas kernels: none -> 74.1 us  [fused_body(): pl.pallas_call(lambda *refs: fused_kernel(grad_scale, *refs), out_shape=(...]
    all_gather x3 -> x0, blocking collectives: 73.2 us -> none  [the longest x1 33.4 us: body(): lax.all_gather(point_weight, 'seq', axis=0, tiled=True)]
    reduce_scatter x1 -> x0, waiting for transfers between devices: 71.7 us -> none  [body(): lax.psum_scatter(conv_terms, 'dp', scatter_dimension=1, tiled=True)]
    dot_general x10 -> x0, matrix products: 32.5 us -> none  [the longest x7 24.9 us: product(): return jnp.dot(left, right, preferred_element_type=jnp.float32)]
    ppermute x4 -> x0, starting transfers between devices: 14.9 us -> none  [from_behind(): return lax.ppermute(x, axis, pairs)]
    unnamed x4 -> x0, waiting for transfers between devices: 13.8 us -> none
    ppermute x4 -> x0, waiting for transfers between devices: 7.37 us -> none  [from_behind(): return lax.ppermute(x, axis, pairs)]
    convert_element_type x3 -> x0, other arithmetic: 5.53 us -> none  [the longest x1 2.38 us: body(): acted = gelu_tanh(normed).astype(jnp.bfloat16)]
  transfers between devices with their start and end apart: 7 -> 0, of which waited for: 3 -> 0; matrix products, arithmetic and copies ran while one was open for 13% -> 0% of each run, Pallas kernels for 0% -> 0%
where the time goes in v2:
time: 78.3 us; the launch traced here: 78.1 us
  Pallas kernels  74.1 us (95%)
  local copies, waits for them, and re-layouts  3.35 us (4%)
    pallas_call x1, Pallas kernels, fused_body(): pl.pallas_call(lambda *refs: fused_kernel(grad_scale, *refs), out_shape=(...  74.1 us
    unnamed x4, local copies, waits for them, and re-layouts  3.35 us

profile of v2, /device:TPU:0, one launch (start us, length us, event | category | flops | bytes accessed | tf_op | source)
XLA Modules:
  0.0 78.1 jit_solution(727872581636839542)
XLA Ops:
  0.6 74.1 %shard_map.59 = (bf16[1024,768]{1,0:T(8,128)(2,1)}, f32[3,96,96]{2,1,0:T(8,128)}) custom-call(bf16[1024,768]{1,0:T(8,128)(2,1)} %bitcast.3, bf16[3,96,96]{2,1,0:T(8,128)(2,1)} %refs_1_.1, bf16[96,96]{1,0:T(8,128)(2,1)} %refs_2_.1, bf16[1024,768]{1,0:T(8,128)(2,1)} %bitcast.4), custom_call_target="tpu_custom_call" | custom-call | tf_op jit(solution)/shard_map/pallas_call | solution.py:437
  74.8 0.0 copy-start
  74.8 2.7 %copy.8 = bf16[2,512,768]{2,1,0:T(8,128)(2,1)} copy(bf16[2,512,768]{2,1,0:T(8,128)(2,1)} %bitcast.5) | data formatting | bytes 3145728
  77.5 0.0 copy-done
  77.5 0.7 copy.9
Async XLA Ops:
  74.8 2.7 %copy-start = (f32[3,96,96]{2,1,0:T(8,128)S(1)}, f32[3,96,96]{2,1,0:T(8,128)}, u32[]{:S(2)}) copy-start(f32[3,96,96]{2,1,0:T(8,128)} %get-tuple-element.9) | copy-start | bytes 331780

commit v3 on v2

--- a/solution.py
+++ b/solution.py
@@ -122,8 +122,9 @@
 
 def fused_kernel(
     grad_scale,
-    x_ref, conv_w_ref, point_w_ref, cot_ref,
-    out_ref, conv_ref,
+    x_hbm, conv_w_ref, point_w_ref, cot_hbm,
+    out_hbm, conv_ref,
+    x_ref, cot_ref, out_ref, io_s,
     w_own, w_in, first_w, rest_w, w_halo, w_mid, w_point,
     acted, normed, slope, scale,
     mid, inner, tap_out, tap_in, pre_out, pre_in,
@@ -147,6 +148,10 @@
     def zdev(k):
         return (lax.rem(z + k, ZS) * YS + y, s)
 
+    load_x = pltpu.make_async_copy(x_hbm, x_ref, io_s.at[0])
+    load_cot = pltpu.make_async_copy(cot_hbm, cot_ref, io_s.at[1])
+    load_x.start()
+    load_cot.start()
     barrier = pltpu.get_barrier_semaphore()
     for dev in (sib, xn, yn, zdev(1), zdev(2), zdev(3)):
         pl.semaphore_signal(barrier, inc=1, device_id=dev, device_id_type=MESH)
@@ -193,6 +198,7 @@
          point_w_ref[...].astype(jnp.float32).T.astype(jnp.bfloat16)], axis=1)
     pl.semaphore_wait(barrier, 6)
     send(w_own, w_in, wx_s.at[0], wx_r.at[0], xn)
+    load_x.wait()
     activations(0)
     activations(1)
     arrived(w_in, wx_s.at[0], wx_r.at[0], xn)
@@ -272,10 +278,12 @@
         send(tap_out.at[chunk(q)], tap_in.at[chunk(q)], tp_s.at[q], tp_r.at[q], xn)
 
     tap(0)
+    tap(1)
     for k in ORDER:
         take_z(1, k)
-    for q in range(1, chunks):
-        tap(q)
+    tap(2)
+    tap(3)
+    load_cot.wait()
     for k in (0,) + ORDER:
         take_y(1, k)
     take_core(1)
@@ -320,8 +328,8 @@
         return lax.dot_general(a, b, over_lanes, preferred_element_type=jnp.float32)
 
     def share_core(t):
-        def pack(i, carry):
-            at = pl.ds(pl.multiple_of(i * 64, 16), 64)
+        def pack(start, i):
+            at = pl.ds(pl.multiple_of(start + i * 64, 16), 64)
             g = grads[t, at, :] * grad_scale
             blank = jnp.zeros((64, 256 - 2 * lane), jnp.float32)
 
@@ -332,17 +340,21 @@
             even, odd = columns(0), columns(1)
             own[t, at, :] = jnp.where(c == 0, even, odd)
             sib_out[t, at, :] = jnp.where(c == 0, odd, even).astype(jnp.bfloat16)
-            return carry
-
-        lax.fori_loop(0, width // 64, pack, 0)
-        send(sib_out.at[t], sib_in.at[t], cs_s.at[t], cs_r.at[t], sib)
+
+        for k in ORDER + (0,):
+            start = lax.rem(z + k, ZS) * (YS * part)
+            for i in range(YS * part // 64):
+                pack(start, i)
+            at = pl.ds(pl.multiple_of(start, 16), YS * part)
+            send(sib_out.at[t, at], sib_in.at[t, at], cs_s.at[t, k], cs_r.at[t, k], sib)
 
     def dest(k, yy):
         return pl.ds(pl.multiple_of((lax.rem(z + k, ZS) * YS + yy) * part, 16), part)
 
     def share_y(t):
-        arrived(sib_in.at[t], cs_s.at[t], cs_r.at[t], sib)
         for k in ORDER + (0,):
+            start = pl.multiple_of(lax.rem(z + k, ZS) * (YS * part), 16)
+            arrived(sib_in.at[t, pl.ds(start, YS * part)], cs_s.at[t, k], cs_r.at[t, k], sib)
             at = dest(k, 1 - y)
             y_out[t, k] = (own[t, at, :] + sib_in[t, at, :].astype(jnp.float32)).astype(jnp.bfloat16)
             send(y_out.at[t, k], y_in.at[t, k], cy_s.at[t, k], cy_r.at[t, k], yn)
@@ -368,6 +380,9 @@
         x_out[t] = total.astype(jnp.bfloat16)
         send(x_out.at[t], x_in.at[t], cx_s.at[t], cx_r.at[t], xn)
 
+    def store(q):
+        return pltpu.make_async_copy(out_ref.at[chunk(q)], out_hbm.at[chunk(q)], io_s.at[2 + q])
+
     def finish(q):
         act = back(pre_in[chunk(q), :], w_halo[...]) + back(pre_out[chunk(q), :], w_mid[...])
         slope[chunk(q), :] = act * slope[chunk(q), :]
@@ -382,6 +397,7 @@
             return carry
 
         lax.fori_loop(0, size // step, one, 0)
+        store(q).start()
 
     def halo_term(q):
         arrived(pre_in.at[chunk(q)], gp_s.at[q], gp_r.at[q], xn)
@@ -398,13 +414,13 @@
     share_x(1)
     finish(1)
     halo_term(2)
+    finish(2)
     halo_term(3)
     share_core(0)
     share_y(0)
     share_z(0)
-    finish(2)
+    finish(3)
     share_x(0)
-    finish(3)
 
     def pick(v):
         return jnp.where(is_low, v[:, :lane], v[:, lane:2 * lane])
@@ -417,6 +433,20 @@
     conv_ref[2] = jnp.where(is_low, their_halo, own_halo)
     for copy in pending:
         copy.wait_send()
+    for q in range(chunks):
+        store(q).wait()
+
+
+def hand_over(grad_ref, conv_ref, grad_out, conv_out, sem):
+    size = grad_ref.shape[0] // 8
+    copies = [pltpu.make_async_copy(conv_ref, conv_out, sem.at[8])]
+    for i in range(8):
+        at = pl.ds(i * size, size)
+        copies.append(pltpu.make_async_copy(grad_ref.at[at], grad_out.at[at], sem.at[i]))
+    for copy in copies:
+        copy.start()
+    for copy in copies:
+        copy.wait()
 
 
 def fused_body(inputs, conv_weight, point_weight, cotangent):
@@ -434,15 +464,19 @@
         return [pltpu.SemaphoreType.DMA(n)] * 2
 
     whole = pl.BlockSpec(memory_space=pltpu.VMEM)
+    away = pl.BlockSpec(memory_space=pl.ANY)
+    shapes = (
+        jax.ShapeDtypeStruct((rows, width), bf),
+        jax.ShapeDtypeStruct(conv_weight.shape, f32),
+    )
     grad, conv_grad = pl.pallas_call(
         lambda *refs: fused_kernel(grad_scale, *refs),
-        out_shape=(
-            jax.ShapeDtypeStruct((rows, width), bf),
-            jax.ShapeDtypeStruct(conv_weight.shape, f32),
-        ),
-        in_specs=[whole] * 4,
-        out_specs=(whole, whole),
+        out_shape=shapes,
+        in_specs=[away, whole, whole, away],
+        out_specs=(away, whole),
         scratch_shapes=[
+            vmem(bf, rows, width), vmem(bf, rows, width), vmem(bf, rows, width),
+            pltpu.SemaphoreType.DMA((6,)),
             vmem(bf, part, hidden), vmem(bf, part, hidden),
             vmem(bf, 2, width, 256), vmem(bf, 2, width, hidden),
             vmem(bf, width, hidden), vmem(bf, width, hidden), vmem(bf, width, hidden),
@@ -456,11 +490,19 @@
             vmem(bf, 2, 4, part, 256), vmem(bf, 2, 4, part, 256),
             vmem(f32, 2, part, 256), vmem(bf, 2, part, 256), vmem(bf, 2, part, 256),
             *sems(1), *sems(2, 4), *sems(2, 4), *sems(2, 8),
-            *sems(4), *sems(4), *sems(2), *sems(2, 4), *sems(2, 4), *sems(2),
+            *sems(4), *sems(4), *sems(2, 4), *sems(2, 4), *sems(2, 4), *sems(2),
         ],
         compiler_params=pltpu.CompilerParams(
             collective_id=0, has_side_effects=True, vmem_limit_bytes=56 * 1024 * 1024),
     )(inputs.reshape(rows, width), conv_weight, point_weight, cotangent.reshape(rows, width))
+    grad, conv_grad = pl.pallas_call(
+        hand_over,
+        out_shape=shapes,
+        in_specs=[away, away],
+        out_specs=(away, away),
+        scratch_shapes=[pltpu.SemaphoreType.DMA((9,))],
+        compiler_params=pltpu.CompilerParams(vmem_limit_bytes=56 * 1024 * 1024),
+    )(grad, conv_grad)
     return grad.reshape(samp_count, bin_count, width), conv_grad
 
 

time: 78.3 us -> 126 us (1.61)
  Pallas kernels: 74.1 us -> 125 us
  local copies, waits for them, and re-layouts: 3.35 us -> 0 us
    pallas_call x1 -> x2, Pallas kernels: 74.1 us -> 125 us  [the longest x1 71.5 us: fused_body(): pl.pallas_call(lambda *refs: fused_kernel(grad_scale, *refs), out_shape=s...]
    unnamed x4 -> x0, local copies, waits for them, and re-layouts: 3.35 us -> none
where the time goes in v3:
time: 126 us; the launch traced here: 125 us
  Pallas kernels  125 us (99%)
    pallas_call x1, Pallas kernels, fused_body(): pl.pallas_call(lambda *refs: fused_kernel(grad_scale, *refs), out_shape=s...  71.5 us
    pallas_call x1, Pallas kernels, fused_body(): pl.pallas_call(hand_over, out_shape=shapes, in_specs=[away, away], out_sp...  53.3 us

profile of v3, /device:TPU:0, one launch (start us, length us, event | category | flops | bytes accessed | tf_op | source)
XLA Modules:
  0.0 125.5 jit_solution(14713485782226663182)
XLA Ops:
  0.6 71.5 %shard_map.59 = (bf16[1024,768]{1,0:T(8,128)(2,1)}, f32[3,96,96]{2,1,0:T(8,128)}) custom-call(bf16[1024,768]{1,0:T(8,128)(2,1)} %bitcast.3, bf16[3,96,96]{2,1,0:T(8,128)(2,1)} %refs_1_.1, bf16[96,96]{1,0:T(8,128)(2,1)} %refs_2_.1, bf16[1024,768]{1,0:T(8,128)(2,1)} %bitcast.4), custom_call_target="tpu_custom_call" | custom-call | tf_op jit(solution)/shard_map/pallas_call | solution.py:472
  72.2 53.3 %shard_map.60 = (bf16[1024,768]{1,0:T(8,128)(2,1)}, f32[3,96,96]{2,1,0:T(8,128)}) custom-call(bf16[1024,768]{1,0:T(8,128)(2,1)} %get-tuple-element.6.grad_ref, f32[3,96,96]{2,1,0:T(8,128)} %get-tuple-element.7.conv_ref), custom_call_target="tpu_custom_call" | custom-call | tf_op jit(solution)/shard_map/pallas_call | solution.py:498
